TPU v7x, 32 devices: a whole 2x2x4 slice. The times are simulated.
32 devices in a mesh: groups: 2 (over y), inst: 4 (over z), tp: 4 (over x, core).
Axes of the slice: x: 2, y: 2, z: 4, core: 2. Of those that a mesh axis runs over, the one named last changes fastest.
Arguments:
- kv_pool: bfloat16 [128, 2, 512, 1024], P(('groups', 'inst'), None, None, 'tp'), parts along dimension 0, may hold values from -16 to 16
- page_table: int32 [64, 8], P(('groups', 'inst')), parts along dimension 0, may hold values from 0 to 15, as said below
- lengths: int32 [64], P(('groups', 'inst')), parts along dimension 0, may hold values from 1 to 4096, as said below
- queries: bfloat16 [64, 2, 8192], P(('groups', 'inst'), None, 'tp'), parts along dimension 0, may hold values from -8 to 8
- new_kv: bfloat16 [64, 2, 2, 1024], P(('groups', 'inst'), None, None, 'tp'), parts along dimension 0, may hold values from -6 to 6
- moves: int32 [8, 2], P('groups'), parts along dimension 0, may hold values from 0 to 31, as said below
Outputs:
- attended: bfloat16 [64, 2, 8192], P(('groups', 'inst'), None, 'tp'), parts along dimension 0
There are 2 independent parts, one for each index of `groups`. A program takes and returns all parts, laid end to end along the dimension named above; each array names one. Nothing has to cross between parts.
Inputs may be any that keep to these rules, and one draw needn't show every extreme that they name: Slot i holds ceil(lengths[i] / 512) cache blocks, listed first in its page table; the blocks of the slots of one instance are distinct; some slot holds exactly 4096 tokens. `page_table`: entries past a slot's block count are valid block numbers of the same pool. The two entries of a move lie on different instances; no slot appears twice in the list; half of the instances hold the cache slots of exactly 2 moves and no hidden slot, the other half exactly 2 hidden slots and no cache slot; no two moves join the same pair of instances.
All inputs are finite; a program needn't handle non-finite values.
Results may differ from a plain program's by a relative error of at most 0.0025.
Values may be sent and summed in bfloat16 or wider, within the bound.
No kernel may reach another device: no remote copies, remote signals or barrier semaphores. Data moves between devices by JAX's collectives and lax.ppermute only.
A program may use at most 64 MiB of HBM per device.

v0:
```python
import math

import jax
import jax.numpy as jnp
from jax import lax
from jax.sharding import PartitionSpec as P

HD = 128
CAP = 2


def attend_rows(kv_pool, query_rows, fresh_rows, page_rows, length_rows):
    slot_count = kv_pool.shape[0]
    block_size = kv_pool.shape[2]
    columns = kv_pool.shape[3]
    groups = columns // HD
    row_count = query_rows.shape[0]
    steps_count = query_rows.shape[1]
    per_group = query_rows.shape[2] // (groups * HD)
    page_count = page_rows.shape[1]
    token_count = slot_count * block_size
    cache_keys = kv_pool[:, 0].reshape(token_count, groups, HD)
    cache_values = kv_pool[:, 1].reshape(token_count, groups, HD)
    fresh_keys = fresh_rows[:, :, 0].reshape(row_count, steps_count, groups, HD)
    fresh_values = fresh_rows[:, :, 1].reshape(row_count, steps_count, groups, HD)
    query_heads = query_rows.reshape(row_count, steps_count, groups, per_group, HD)
    block_total = (length_rows + block_size - 1) // block_size
    page_ids = jnp.arange(page_count)
    live = page_ids[None, :] < block_total[:, None]
    match = (page_rows[:, :, None] == jnp.arange(slot_count)[None, None, :]) & live[:, :, None]
    owned = jnp.any(match, axis=1)
    place = jnp.sum(jnp.where(match, page_ids[None, :, None], 0), axis=1)
    offsets = place[:, :, None] * block_size + jnp.arange(block_size)[None, None, :]
    in_range = (owned[:, :, None] & (offsets < length_rows[:, None, None])).reshape(
        row_count, token_count
    )
    score_scale = 1.0 / math.sqrt(HD)
    cached = (
        jnp.einsum("rsgqd,tgd->rsgqt", query_heads, cache_keys, preferred_element_type=jnp.float32)
        * score_scale
    )
    recent = (
        jnp.einsum("rsgqd,rugd->rsgqu", query_heads, fresh_keys, preferred_element_type=jnp.float32)
        * score_scale
    )
    step_order = (jnp.arange(steps_count)[None, :] <= jnp.arange(steps_count)[:, None])[
        None, :, None, None, :
    ]
    cached = jnp.where(in_range[:, None, None, None, :], cached, -1e30)
    recent = jnp.where(step_order, recent, -1e30)
    row_max = jnp.maximum(
        jnp.max(cached, axis=4, keepdims=True), jnp.max(recent, axis=4, keepdims=True)
    )
    cached_exp = jnp.exp(cached - row_max)
    recent_exp = jnp.exp(recent - row_max)
    denominator = jnp.sum(cached_exp, axis=4) + jnp.sum(recent_exp, axis=4)
    weighted = jnp.einsum(
        "rsgqt,tgd->rsgqd",
        cached_exp.astype(jnp.bfloat16),
        cache_values,
        preferred_element_type=jnp.float32,
    )
    weighted = weighted + jnp.einsum(
        "rsgqu,rugd->rsgqd",
        recent_exp.astype(jnp.bfloat16),
        fresh_values,
        preferred_element_type=jnp.float32,
    )
    result = (weighted / denominator[..., None]).astype(jnp.bfloat16)
    return result.reshape(row_count, steps_count, groups * per_group * HD)


def select_sum(selector, values):
    return jnp.sum(jnp.where(selector, values[None, :], 0), axis=1)


def body(kv_pool, page_table, lengths, queries, new_kv, moves):
    rows_inst = page_table.shape[0]
    move_count = moves.shape[0]
    this_inst = lax.axis_index("inst")
    cache_slot = moves[:, 0]
    hidden_slot = moves[:, 1]
    from_inst = cache_slot // rows_inst
    to_inst = hidden_slot // rows_inst
    move_ids = jnp.arange(move_count)
    earlier = move_ids[None, :] < move_ids[:, None]
    rank_to = jnp.sum(earlier & (to_inst[None, :] == to_inst[:, None]), axis=1)
    rank_from = jnp.sum(earlier & (from_inst[None, :] == from_inst[:, None]), axis=1)
    rank_ids = jnp.arange(CAP)
    mine_to = (to_inst[None, :] == this_inst) & (rank_to[None, :] == rank_ids[:, None])
    mine_from = (from_inst[None, :] == this_inst) & (rank_from[None, :] == rank_ids[:, None])
    held_valid = jnp.any(mine_to, axis=1)
    owned_valid = jnp.any(mine_from, axis=1)
    held_local = select_sum(mine_to, hidden_slot % rows_inst)
    owned_local = select_sum(mine_from, cache_slot % rows_inst)
    held_q = jnp.take(queries, held_local, axis=0)
    held_kv = jnp.take(new_kv, held_local, axis=0)
    slot_ids = jnp.arange(rows_inst)
    gathered_q, gathered_kv = (
        lax.all_gather(held_q, "inst", axis=0, tiled=True),
        lax.all_gather(held_kv, "inst", axis=0, tiled=True),
    )
    owned_index = select_sum(mine_from, to_inst * CAP + rank_to)
    owned_q = jnp.take(gathered_q, owned_index, axis=0)
    owned_kv = jnp.take(gathered_kv, owned_index, axis=0)
    owned_hit = (owned_local[:, None] == slot_ids[None, :]) & owned_valid[:, None]
    vacated = jnp.any(owned_hit, axis=0)
    owned_which = jnp.sum(jnp.where(owned_hit, rank_ids[:, None], 0), axis=0)
    query_use = jnp.where(vacated[:, None, None], jnp.take(owned_q, owned_which, axis=0), queries)
    fresh_use = jnp.where(
        vacated[:, None, None, None], jnp.take(owned_kv, owned_which, axis=0), new_kv
    )
    local_out = attend_rows(kv_pool, query_use, fresh_use, page_table, lengths)
    owned_out = jnp.take(local_out, owned_local, axis=0)
    gathered_out = lax.all_gather(owned_out, "inst", axis=0, tiled=True)
    held_index = select_sum(mine_to, from_inst * CAP + rank_from)
    held_out = jnp.take(gathered_out, held_index, axis=0)
    held_hit = (held_local[:, None] == slot_ids[None, :]) & held_valid[:, None]
    arrived = jnp.any(held_hit, axis=0)
    held_which = jnp.sum(jnp.where(held_hit, rank_ids[:, None], 0), axis=0)
    result = jnp.where(arrived[:, None, None], jnp.take(held_out, held_which, axis=0), local_out)
    return jnp.where(vacated[:, None, None], jnp.zeros_like(result), result)


def solution(mesh):
    placed = (
        P(("groups", "inst"), None, None, "tp"),
        P(("groups", "inst"), None),
        P(("groups", "inst")),
        P(("groups", "inst"), None, "tp"),
        P(("groups", "inst"), None, None, "tp"),
        P("groups", None),
    )
    return jax.shard_map(
        body,
        mesh=mesh,
        in_specs=placed,
        out_specs=P(("groups", "inst"), None, "tp"),
        check_vma=False,
    )
```

profile of v0, /device:TPU:0, one launch (start us, length us, event | category | flops | bytes accessed | tf_op | source)
XLA Modules:
  0.0 88.9 jit_solution(18380320686762328972)
XLA Ops:
  0.0 0.8 and_select_fusion.1
  0.8 0.8 broadcast_compare_fusion
  1.5 0.8 fusion.34
  2.3 0.2 convert_reduce_fusion.1
  2.5 0.1 fusion.36
  2.6 0.2 convert_reduce_fusion
  2.8 0.2 select_reduce_fusion.2
  3.0 0.1 fusion.32
  3.1 5.8 %fusion.38 = (bf16[16,1,512,256]{3,2,1,0:T(8,128)(2,1)}, bf16[16,1,512,256]{3,2,1,0:T(8,128)(2,1)}) fusion(bf16[16,2,512,256]{3,2,1,0:T(8,128)(2,1)} %param.12), kind=kLoop, calls=%fused_computation.132 | loop fusion | bytes 16777216 | tf_op jit(solution)/shard_map/slice | solution.py:22
  8.9 7.0 %reshape.376 = bf16[8192,2,128]{2,1,0:T(2,128)(2,1)} reshape(bf16[16,1,512,256]{3,2,1,0:T(8,128)(2,1)} %get-tuple-element.23) | data formatting | bytes 8388608 | tf_op jit(solution)/shard_map/reshape;squeeze | solution.py:23
  15.9 6.9 %reshape.374 = bf16[8192,2,128]{2,1,0:T(2,128)(2,1)} reshape(bf16[16,1,512,256]{3,2,1,0:T(8,128)(2,1)} %get-tuple-element.22) | data formatting | bytes 8388608 | tf_op jit(solution)/shard_map/reshape;squeeze | solution.py:22
  22.8 0.6 gather_fusion.1
  23.4 0.1 broadcast_select_fusion.9
  23.5 14.9 %all_gather.9 = bf16[8,2,2048]{2,1,0:T(2,128)(2,1)S(1)} all-gather(bf16[2,2,2048]{2,1,0:T(2,128)(2,1)S(1)} %broadcast_select_fusion.9), channel_id=1, replica_groups=mesh['groups'=2,'inst'=4,'tp'=4] {'inst'}, dimensions={0}, use_global_device_ids=true | all-gather | bytes 81920 | tf_op jit(solution)/shard_map/all_gather | solution.py:100
  38.4 0.6 gather_fusion.2
  39.0 0.1 broadcast_select_fusion.8
  39.1 0.1 select_reduce_fusion.3
  39.2 0.7 gather_fusion.3
  39.9 0.2 broadcast_select_fusion.4
  40.3 0.1 fusion.23
  40.4 0.1 copy.92
  40.4 0.1 and.184
  40.5 0.1 select_reduce_fusion
  40.7 0.1 add.120
  40.8 0.1 fusion.19
  41.0 7.5 %fusion.40 = (f32[8,2,2,8]{3,1,0,2:T(2,128)S(1)}, f32[8,2,2,8,8192]{4,3,1,0,2:T(8,128)}) fusion(bf16[8192,2,128,1,1]{2,1,0,4,3:T(2,128)(2,1)} %bitcast.66, bf16[8,2,2,8,128]{4,3,2,1,0:T(8,128)(2,1)S(1)} %reshape.272, pred[8,8192]{1,0:T(8,128)(4,1)S(1)} %fusion.19), kind=kOutput, calls=%fused_computation.134 | convolution fusion | flops 543162112 | bytes 12715008 | tf_op jit(solution)/shard_map/rsgqd,tgd->rsgqt/dot_general | solution.py:39
  48.5 0.6 gather_fusion.4
  49.0 0.1 broadcast_select_fusion.12
  49.1 13.1 %all_gather.10 = bf16[8,2,2,256]{3,2,1,0:T(2,128)(2,1)S(1)} all-gather(bf16[2,2,2,256]{3,2,1,0:T(2,128)(2,1)S(1)} %broadcast_select_fusion.12), channel_id=1, replica_groups=mesh['groups'=2,'inst'=4,'tp'=4] {'inst'}, dimensions={0}, use_global_device_ids=true | all-gather | bytes 20480 | tf_op jit(solution)/shard_map/all_gather | solution.py:101
  62.2 0.6 gather_fusion.5
  62.8 0.1 broadcast_select_fusion.11
  62.9 0.6 gather_fusion
  63.5 0.1 broadcast_select_fusion.5
  63.6 0.1 slice_reduce_fusion
  63.7 0.4 fusion.39
  64.2 6.4 %fusion.9 = f32[8,2,2,8,128]{4,3,1,0,2:T(8,128)S(1)} fusion(bf16[8192,2,128,1,1]{2,1,0,4,3:T(2,128)(2,1)} %bitcast.65, f32[8,2,2,8,8192]{4,3,1,0,2:T(8,128)} %get-tuple-element.35, f32[8,2,2,8]{3,1,0,2:T(2,128)S(1)} %copy.102), kind=kOutput, calls=%fused_computation.19 | convolution fusion | flops 541065216 | bytes 12715008 | tf_op jit(solution)/shard_map/rsgqt,tgd->rsgqd/dot_general | solution.py:57
  70.7 1.3 %fusion.2 = f32[8,2,2,8]{3,1,0,2:T(2,128)S(1)} fusion(f32[8,2,2,8,8192]{4,3,1,0,2:T(8,128)S(1)} %copy-done, f32[8,2,2,8]{3,1,0,2:T(2,128)S(1)} %copy.102), kind=kLoop, calls=%fused_computation.13 | loop fusion | flops 4194048 | bytes 8390656 | tf_op jit(solution)/shard_map/reduce_sum | solution.py:56
  72.2 0.2 fusion.16
  72.5 0.6 gather_fusion.6
  73.1 0.1 broadcast_select_fusion.7
  73.2 13.1 %all_gather.11 = bf16[8,2,2048]{2,1,0:T(2,128)(2,1)S(1)} all-gather(bf16[2,2,2048]{2,1,0:T(2,128)(2,1)S(1)} %broadcast_select_fusion.7), channel_id=1, replica_groups=mesh['groups'=2,'inst'=4,'tp'=4] {'inst'}, dimensions={0}, use_global_device_ids=true | all-gather | bytes 81920 | tf_op jit(solution)/shard_map/all_gather | solution.py:115
  86.3 0.6 gather_fusion.7
  86.9 0.1 broadcast_select_fusion.6
  87.0 0.1 fusion.37
  87.1 0.1 select_reduce_fusion.1
  87.2 0.7 gather_fusion.8
  87.9 0.1 fusion.31
  88.0 0.9 broadcast_select_fusion.3
  (49 shorter events, 0.6 us)
Async XLA Ops:
  8.9 13.9 %copy-start.1 = (bf16[8,2,2048]{2,1,0:T(2,128)(2,1)S(1)}, bf16[8,2,2048]{2,1,0:T(2,128)(2,1)}, u32[]{:S(2)}) copy-start(bf16[8,2,2048]{2,1,0:T(2,128)(2,1)} %param.15) | copy-start | bytes 196612
  8.9 31.3 %copy-start.4 = (s32[8]{0:T(128)S(1)}, s32[8]{0:T(128)}, u32[]{:S(2)}) copy-start(s32[8]{0:T(128)} %param.14) | copy-start | bytes 100
  8.9 31.4 %copy-start.3 = (s32[8,8]{1,0:T(8,128)S(1)}, s32[8,8]{1,0:T(8,128)}, u32[]{:S(2)}) copy-start(s32[8,8]{1,0:T(8,128)} %param.13) | copy-start | bytes 772
  40.4 8.0 %copy-start.2 = (bf16[8,2,2,256]{3,2,1,0:T(2,128)(2,1)S(1)}, bf16[8,2,2,256]{3,2,1,0:T(2,128)(2,1)}, u32[]{:S(2)}) copy-start(bf16[8,2,2,256]{3,2,1,0:T(2,128)(2,1)} %param.16) | copy-start | bytes 49156
  63.7 7.0 %copy-start = (f32[8,2,2,8,8192]{4,3,1,0,2:T(8,128)S(1)}, f32[8,2,2,8,8192]{4,3,1,0,2:T(8,128)}, u32[]{:S(2)}) copy-start(f32[8,2,2,8,8192]{4,3,1,0,2:T(8,128)} %get-tuple-element.35) | copy-start | bytes 25165828
where the time goes:
time: 89.4 us; the launch traced here: 88.9 us
  blocking collectives  41.2 us (46%)
  local copies, waits for them, and re-layouts  25.8 us (29%)
  matrix products  14.5 us (16%)
  other arithmetic  7.05 us (8%)
    all_gather x1, blocking collectives, body(): lax.all_gather(held_q, 'inst', axis=0, tiled=True)  14.9 us
    all_gather x1, blocking collectives, body(): lax.all_gather(held_kv, 'inst', axis=0, tiled=True)  13.1 us
    all_gather x1, blocking collectives, body(): gathered_out = lax.all_gather(owned_out, 'inst', axis=0, tiled=True)  13.1 us
    dot_general x1, matrix products, attend_rows(): jnp.einsum('rsgqd,tgd->rsgqt', query_heads, cache_keys, preferred_element...  7.47 us
    another operation x1, local copies, waits for them, and re-layouts, attend_rows(): cache_values = kv_pool[:, 1].reshape(token_count, groups, HD)  6.98 us
    another operation x1, local copies, waits for them, and re-layouts, attend_rows(): cache_keys = kv_pool[:, 0].reshape(token_count, groups, HD)  6.91 us
    dot_general x1, matrix products, attend_rows(): jnp.einsum('rsgqt,tgd->rsgqd', cached_exp.astype(jnp.bfloat16), cache_val...  6.42 us
    slice x1, local copies, waits for them, and re-layouts, attend_rows(): cache_keys = kv_pool[:, 0].reshape(token_count, groups, HD)  5.83 us

commit v1 on v0

v1 whole, which is shorter than its diff:
```python
import functools
import math

import jax
import jax.numpy as jnp
from jax import lax
from jax.experimental import pallas as pl
from jax.experimental.pallas import tpu as pltpu
from jax.sharding import PartitionSpec as P

HD = 128
NEG = -1e30
SMEM = pltpu.SMEM
VMEM = pltpu.VMEM
ANY = pl.ANY


def find_moves(moves, rows_inst, n, me, hidden, cache):
    for d in range(n):
        if hidden is not None:
            hidden[d] = -1
        if cache is not None:
            cache[d] = -1

    def step(m, carry):
        cache_slot = moves[m, 0]
        hidden_slot = moves[m, 1]
        from_inst = cache_slot // rows_inst
        to_inst = hidden_slot // rows_inst
        shift = lax.rem(from_inst - to_inst + n, n)
        if hidden is not None:
            hidden[jnp.where(to_inst == me, shift, 0)] = lax.rem(hidden_slot, rows_inst)
        if cache is not None:
            cache[jnp.where(from_inst == me, shift, 0)] = lax.rem(cache_slot, rows_inst)
        return carry

    lax.fori_loop(0, moves.shape[0], step, 0)


def pack_kernel(n, moves, q, kv, *refs):
    outs, hidden = refs[: n - 1], refs[n - 1]
    rows_inst = q.shape[0]
    heads = q.shape[1]
    me = lax.axis_index("inst")
    find_moves(moves, rows_inst, n, me, hidden, None)
    for d in range(1, n):
        slot = jnp.maximum(hidden[d], 0)
        outs[d - 1][0:heads, :] = q[slot]
        outs[d - 1][heads:, :] = kv[slot]


def attend_kernel(n, moves, page_table, lengths, q, kv, pool, *refs):
    recv = refs[: n - 1]
    out = refs[n - 1]
    back = refs[n : 2 * n - 1]
    (cache, owner, limit, vacant, buf, qbd, fk, scores, part_max, top, part_sum, acc, sems) = refs[2 * n - 1 :]
    rows_inst, heads, hd = q.shape
    fresh_rows = kv.shape[1]
    slots, _, block, columns = pool.shape
    groups = columns // hd
    steps = fresh_rows // (2 * groups)
    per = heads // groups
    pages = page_table.shape[1]
    me = lax.axis_index("inst")
    scale = 1.0 / math.sqrt(hd)

    def fetch(p, plane):
        return pltpu.make_async_copy(pool.at[p, plane], buf.at[p, plane], sems.at[p, plane])

    for plane in range(2):
        for p in range(slots):
            fetch(p, plane).start()

    find_moves(moves, rows_inst, n, me, None, cache)
    for p in range(slots + 1):
        owner[p] = rows_inst
        limit[p] = 0
    for r in range(rows_inst):
        length = lengths[r]
        vacant[r] = 0
        for b in range(pages):
            at = jnp.where(b * block < length, page_table[r, b], slots)
            owner[at] = r
            limit[at] = length - b * block

    zero = jnp.zeros((per, hd), jnp.bfloat16)

    def set_row(r, rows, fresh):
        for g in range(groups):
            for k in range(groups):
                qbd[r, g * per : (g + 1) * per, k * hd : (k + 1) * hd] = (
                    rows[g * per : (g + 1) * per] if k == g else zero
                )
        fk[r] = fresh.astype(jnp.float32)

    for r in range(rows_inst):
        set_row(r, q[r], kv[r])
    set_row(rows_inst, q[0], kv[0])
    for d in range(1, n):

        @pl.when(cache[d] >= 0)
        def _():
            slot = cache[d]
            set_row(slot, recv[d - 1][0:heads, :], recv[d - 1][heads:, :])
            vacant[slot] = 1

    step_of = lax.broadcasted_iota(jnp.int32, (per, 1), 0) % steps
    fresh_scores = []
    for r in range(rows_inst):
        row_scores = []
        for g in range(groups):
            qg = qbd[r, g * per : (g + 1) * per, g * hd : (g + 1) * hd].astype(jnp.float32)
            line = []
            for u in range(steps):
                key = fk[r, pl.ds((u * groups + g) * 2, 1), :]
                s = jnp.sum(qg * key, axis=1, keepdims=True)
                line.append(jnp.where(step_of >= u, s, NEG))
            row_scores.append(line)
        fresh_scores.append(row_scores)
        first = jnp.concatenate(
            [functools.reduce(jnp.maximum, row_scores[g]) for g in range(groups)], axis=0
        )
        part_max[r] = jnp.broadcast_to(first, (heads, hd))
    part_max[rows_inst] = jnp.zeros((heads, hd), jnp.float32)

    lane = lax.broadcasted_iota(jnp.int32, (heads, block), 1)
    for p in range(slots):
        fetch(p, 0).wait()
        r = owner[p]
        s = lax.dot_general(
            qbd[r], buf[p, 0], (((1,), (1,)), ((), ())), preferred_element_type=jnp.float32
        )
        s = jnp.where(lane < limit[p], s, NEG)
        scores[p] = s
        m = part_max[r]
        for c in range(block // hd):
            m = jnp.maximum(m, s[:, c * hd : (c + 1) * hd])
        part_max[r] = m

    factor = scale * math.log2(math.e)
    for r in range(rows_inst):
        m = jnp.max(part_max[r], axis=1, keepdims=True)
        top[r] = jnp.broadcast_to(m, (heads, hd))
        for g in range(groups):
            mg = m[g * per : (g + 1) * per]
            total = jnp.zeros((per, 1), jnp.float32)
            value = jnp.zeros((per, hd), jnp.float32)
            for u in range(steps):
                e = jnp.exp2((fresh_scores[r][g][u] - mg) * factor)
                total = total + e
                weight = e.astype(jnp.bfloat16).astype(jnp.float32)
                value = value + weight * fk[r, pl.ds((u * groups + g) * 2 + 1, 1), :]
            acc[r, g * per : (g + 1) * per, :] = value
            first_lane = lax.broadcasted_iota(jnp.int32, (per, hd), 1) == 0
            part_sum[r, g * per : (g + 1) * per, :] = jnp.where(first_lane, total, 0.0)
    top[rows_inst] = jnp.zeros((heads, hd), jnp.float32)
    part_sum[rows_inst] = jnp.zeros((heads, hd), jnp.float32)
    acc[rows_inst] = jnp.zeros((heads, hd), jnp.float32)

    for p in range(slots):
        fetch(p, 1).wait()
        r = owner[p]
        m = top[r]
        pieces = []
        total = part_sum[r]
        for c in range(block // hd):
            e = jnp.exp2((scores[p, :, c * hd : (c + 1) * hd] - m) * factor)
            total = total + e
            pieces.append(e.astype(jnp.bfloat16))
        part_sum[r] = total
        weights = jnp.concatenate(pieces, axis=1)
        o = lax.dot_general(
            weights, buf[p, 1], (((1,), (0,)), ((), ())), preferred_element_type=jnp.float32
        )
        acc[r] = acc[r] + jnp.concatenate(
            [o[g * per : (g + 1) * per, g * hd : (g + 1) * hd] for g in range(groups)], axis=0
        )

    for r in range(rows_inst):
        total = jnp.sum(part_sum[r], axis=1, keepdims=True)
        value = acc[r] / total
        acc[r] = value
        out[r] = jnp.where(vacant[r] == 1, 0.0, value).astype(jnp.bfloat16)
    for d in range(1, n):
        back[d - 1][...] = acc[jnp.maximum(cache[d], 0)].astype(jnp.bfloat16)


def place_kernel(n, moves, local, *refs):
    back = refs[: n - 1]
    out, hidden = refs[n - 1 :]
    rows_inst = local.shape[0]
    me = lax.axis_index("inst")
    find_moves(moves, rows_inst, n, me, hidden, None)
    out[...] = local[...]
    for d in range(1, n):

        @pl.when(hidden[d] >= 0)
        def _():
            out[hidden[d]] = back[d - 1][...]


def body(kv_pool, page_table, lengths, queries, new_kv, moves):
    n = lax.axis_size("inst")
    rows_inst, steps, width = queries.shape
    columns = kv_pool.shape[3]
    slots, _, block, _ = kv_pool.shape
    groups = columns // HD
    heads_all = width // HD
    heads = steps * heads_all
    fresh_rows = steps * groups * 2
    bf16 = jnp.bfloat16
    f32 = jnp.float32
    q = queries.reshape(rows_inst, steps, heads_all, HD).transpose(0, 2, 1, 3).reshape(rows_inst, heads, HD)
    kv = (
        new_kv.reshape(rows_inst, steps, 2, groups, HD)
        .transpose(0, 1, 3, 2, 4)
        .reshape(rows_inst, fresh_rows, HD)
    )
    smem = pl.BlockSpec(memory_space=SMEM)
    vmem = pl.BlockSpec(memory_space=VMEM)
    anyspace = pl.BlockSpec(memory_space=ANY)
    forward = [[(i, (i + d) % n) for i in range(n)] for d in range(1, n)]
    backward = [[(i, (i - d) % n) for i in range(n)] for d in range(1, n)]

    packed = pl.pallas_call(
        functools.partial(pack_kernel, n),
        out_shape=[jax.ShapeDtypeStruct((heads + fresh_rows, HD), bf16)] * (n - 1),
        in_specs=[smem, vmem, vmem],
        out_specs=[vmem] * (n - 1),
        scratch_shapes=[SMEM((n,), jnp.int32)],
        name="pack",
    )(moves, q, kv)
    received = [lax.ppermute(x, "inst", perm) for x, perm in zip(packed, forward)]
    results = pl.pallas_call(
        functools.partial(attend_kernel, n),
        out_shape=[jax.ShapeDtypeStruct((rows_inst, heads, HD), bf16)]
        + [jax.ShapeDtypeStruct((heads, HD), bf16)] * (n - 1),
        in_specs=[smem, smem, smem, vmem, vmem, anyspace] + [vmem] * (n - 1),
        out_specs=[vmem] * n,
        scratch_shapes=[
            SMEM((n,), jnp.int32),
            SMEM((slots + 1,), jnp.int32),
            SMEM((slots + 1,), jnp.int32),
            SMEM((rows_inst,), jnp.int32),
            VMEM((slots, 2, block, columns), bf16),
            VMEM((rows_inst + 1, heads, columns), bf16),
            VMEM((rows_inst + 1, fresh_rows, HD), f32),
            VMEM((slots, heads, block), f32),
            VMEM((rows_inst + 1, heads, HD), f32),
            VMEM((rows_inst + 1, heads, HD), f32),
            VMEM((rows_inst + 1, heads, HD), f32),
            VMEM((rows_inst + 1, heads, HD), f32),
            pltpu.SemaphoreType.DMA((slots, 2)),
        ],
        compiler_params=pltpu.CompilerParams(vmem_limit_bytes=24 * 1024 * 1024),
        name="attend",
    )(moves, page_table, lengths, q, kv, kv_pool, *received)
    local, back = results[0], results[1:]
    returned = [lax.ppermute(x, "inst", perm) for x, perm in zip(back, backward)]
    out = pl.pallas_call(
        functools.partial(place_kernel, n),
        out_shape=jax.ShapeDtypeStruct((rows_inst, heads, HD), bf16),
        in_specs=[smem, vmem] + [vmem] * (n - 1),
        out_specs=vmem,
        scratch_shapes=[SMEM((n,), jnp.int32)],
        name="place",
    )(moves, local, *returned)
    return out.reshape(rows_inst, heads_all, steps, HD).transpose(0, 2, 1, 3).reshape(rows_inst, steps, width)


def solution(mesh):
    placed = (
        P(("groups", "inst"), None, None, "tp"),
        P(("groups", "inst"), None),
        P(("groups", "inst")),
        P(("groups", "inst"), None, "tp"),
        P(("groups", "inst"), None, None, "tp"),
        P("groups", None),
    )
    return jax.shard_map(
        body,
        mesh=mesh,
        in_specs=placed,
        out_specs=P(("groups", "inst"), None, "tp"),
        check_vma=False,
    )
```

time: 89.4 us -> 39 us (0.44)
  blocking collectives: 41.2 us -> 0 us
  local copies, waits for them, and re-layouts: 25.8 us -> 9.47 us
  matrix products: 14.5 us -> 0 us
  Pallas kernels: 0 us -> 11 us
  starting transfers between devices: 0 us -> 10.7 us
  waiting for transfers between devices: 0 us -> 7.41 us
  other arithmetic: 7.05 us -> 0 us
    all_gather x3 -> x0, blocking collectives: 41.2 us -> none  [the longest x1 14.9 us: body(): lax.all_gather(held_q, 'inst', axis=0, tiled=True)]
    dot_general x4 -> x0, matrix products: 14.5 us -> none  [the longest x1 7.47 us: attend_rows(): jnp.einsum('rsgqd,tgd->rsgqt', query_heads, cache_keys, preferred_element...]
    another operation x4 -> x0, local copies, waits for them, and re-layouts: 13.9 us -> none  [the longest x1 6.98 us: attend_rows(): cache_values = kv_pool[:, 1].reshape(token_count, groups, HD)]
    pallas_call x0 -> x3, Pallas kernels: none -> 11 us  [the longest x1 7.8 us: body(): pl.pallas_call(functools.partial(attend_kernel, n), out_shape=[jax.ShapeD...]
    ppermute x0 -> x6, starting transfers between devices: none -> 10.7 us  [body(): lax.ppermute(x, 'inst', perm)]
    unnamed x12 -> x21, local copies, waits for them, and re-layouts: 0.09 us -> 9.47 us
    ppermute x0 -> x6, waiting for transfers between devices: none -> 7.41 us  [body(): lax.ppermute(x, 'inst', perm)]
    slice x2 -> x0, local copies, waits for them, and re-layouts: 5.91 us -> none  [the longest x1 5.83 us: attend_rows(): cache_keys = kv_pool[:, 0].reshape(token_count, groups, HD)]
  transfers between devices with their start and end apart: 0 -> 6, of which waited for: 0 -> 5; matrix products, arithmetic and copies ran while one was open for 0% -> 0% of each run, Pallas kernels for 0% -> 0%
where the time goes in v1:
time: 39 us; the launch traced here: 38.5 us
  Pallas kernels  11 us (28%)
  starting transfers between devices  10.7 us (27%)
  local copies, waits for them, and re-layouts  9.47 us (24%)
  waiting for transfers between devices  7.41 us (19%)
    ppermute x6, starting transfers between devices, body(): lax.ppermute(x, 'inst', perm)  10.7 us
    unnamed x21, local copies, waits for them, and re-layouts  9.47 us
    pallas_call x1, Pallas kernels, body(): pl.pallas_call(functools.partial(attend_kernel, n), out_shape=[jax.ShapeD...  7.8 us
    ppermute x6, waiting for transfers between devices, body(): lax.ppermute(x, 'inst', perm)  7.41 us
    pallas_call x1, Pallas kernels, body(): pl.pallas_call(functools.partial(place_kernel, n), out_shape=jax.ShapeDty...  1.61 us
    pallas_call x1, Pallas kernels, body(): pl.pallas_call(functools.partial(pack_kernel, n), out_shape=[jax.ShapeDty...  1.55 us
  transfers between devices with their start and end apart: 6, of which 5 were waited for; matrix products, arithmetic and copies ran while one was open for 0% of the time, Pallas kernels for 0%

profile of v1, /device:TPU:0, one launch (start us, length us, event | category | flops | bytes accessed | tf_op | source)
XLA Modules:
  0.0 38.5 jit_solution(9527230548902640316)
XLA Ops:
  0.0 1.3 %copy.11.moves = s32[4,2]{1,0:T(4,128)} copy(s32[4,2]{0,1:T(2,128)} %param.11) | data formatting | bytes 64 | tf_op args[5]
  1.3 1.5 %pack.1 = (bf16[40,128]{1,0:T(8,128)(2,1)}, bf16[40,128]{1,0:T(8,128)(2,1)}, bf16[40,128]{1,0:T(8,128)(2,1)}) custom-call(s32[4,2]{1,0:T(4,128)} %copy.11.moves, bf16[8,32,128]{2,1,0:T(8,128)(2,1)} %bitcast.15, bf16[8,8,128]{2,1,0:T(8,128)(2,1)} %bitcast.17), custom_call_target="tpu_custom_call" | custom-call | tf_op jit(solution)/shard_map/pack/pallas_call | solution.py:225
  2.9 3.0 %collective-permute-start = (bf16[40,128]{1,0:T(8,128)(2,1)}, bf16[40,128]{1,0:T(8,128)(2,1)S(1)}, u32[]{:S(2)}, u32[]{:S(2)}) collective-permute-start(bf16[40,128]{1,0:T(8,128)(2,1)} %get-tuple-element.12), channel_id=1, source_target_pairs={{0,4},{4,8},{8,12},{12,0},{1,5},{5,9},{9,13},{13,1},{2,6},{6,10},{... | collective-permute-start | bytes 30728 | tf_op jit(solution)/shard_map/ppermute | solution.py:233
  5.9 2.6 %collective-permute-start.1 = (bf16[40,128]{1,0:T(8,128)(2,1)}, bf16[40,128]{1,0:T(8,128)(2,1)S(1)}, u32[]{:S(2)}, u32[]{:S(2)}) collective-permute-start(bf16[40,128]{1,0:T(8,128)(2,1)} %get-tuple-element.13), channel_id=1, source_target_pairs={{0,8},{4,12},{8,0},{12,4},{1,9},{5,13},{9,1},{13,5},{2,10},{6,14},... | collective-permute-start | bytes 30728 | tf_op jit(solution)/shard_map/ppermute | solution.py:233
  8.5 1.3 %collective-permute-start.2 = (bf16[40,128]{1,0:T(8,128)(2,1)}, bf16[40,128]{1,0:T(8,128)(2,1)S(1)}, u32[]{:S(2)}, u32[]{:S(2)}) collective-permute-start(bf16[40,128]{1,0:T(8,128)(2,1)} %get-tuple-element.14), channel_id=1, source_target_pairs={{0,12},{4,0},{8,4},{12,8},{1,13},{5,1},{9,5},{13,9},{2,14},{6,2},{... | collective-permute-start | bytes 30728 | tf_op jit(solution)/shard_map/ppermute | solution.py:233
  9.8 0.0 collective-permute-done.refs_0_
  9.8 0.9 %collective-permute-done.1.refs_1_ = bf16[40,128]{1,0:T(8,128)(2,1)S(1)} collective-permute-done((bf16[40,128]{1,0:T(8,128)(2,1)}, bf16[40,128]{1,0:T(8,128)(2,1)S(1)}, u32[]{:S(2)}, u32[]{:S(2)}) %collective-permute-start.1) | collective-permute-done | bytes 10272 | tf_op jit(solution)/shard_map/ppermute | solution.py:233
  10.8 1.6 %collective-permute-done.2.refs_2_ = bf16[40,128]{1,0:T(8,128)(2,1)S(1)} collective-permute-done((bf16[40,128]{1,0:T(8,128)(2,1)}, bf16[40,128]{1,0:T(8,128)(2,1)S(1)}, u32[]{:S(2)}, u32[]{:S(2)}) %collective-permute-start.2) | collective-permute-done | bytes 10272 | tf_op jit(solution)/shard_map/ppermute | solution.py:233
  12.4 0.0 copy-start
  12.4 3.4 %copy-done = bf16[16,2,512,256]{3,2,1,0:T(8,128)(2,1)S(1)} copy-done((bf16[16,2,512,256]{3,2,1,0:T(8,128)(2,1)S(1)}, bf16[16,2,512,256]{3,2,1,0:T(8,128)(2,1)}, u32[]{:S(2)}) %copy-start) | copy-done | bytes 8388632
  15.8 0.0 copy-start.1
  15.8 0.8 %copy-done.1 = bf16[8,2,2048]{2,1,0:T(2,128)(2,1)S(1)} copy-done((bf16[8,2,2048]{2,1,0:T(2,128)(2,1)S(1)}, bf16[8,2,2048]{2,1,0:T(2,128)(2,1)}, u32[]{:S(2)}) %copy-start.1) | copy-done | bytes 65560
  16.6 0.0 copy-start.2
  16.6 0.7 %copy-done.2 = bf16[8,2,2,256]{3,2,1,0:T(2,128)(2,1)S(1)} copy-done((bf16[8,2,2,256]{3,2,1,0:T(2,128)(2,1)S(1)}, bf16[8,2,2,256]{3,2,1,0:T(2,128)(2,1)}, u32[]{:S(2)}) %copy-start.2) | copy-done | bytes 16408
  17.3 0.0 copy-start.4
  17.3 0.7 %copy-done.4 = s32[4,2]{1,0:T(4,128)S(1)} copy-done((s32[4,2]{1,0:T(4,128)S(1)}, s32[4,2]{1,0:T(4,128)}, u32[]{:S(2)}) %copy-start.4) | copy-done | bytes 56
  18.0 0.0 copy-start.5
  18.0 0.7 %copy-done.5 = s32[8,8]{1,0:T(8,128)S(1)} copy-done((s32[8,8]{1,0:T(8,128)S(1)}, s32[8,8]{1,0:T(8,128)}, u32[]{:S(2)}) %copy-start.5) | copy-done | bytes 280
  18.6 0.0 copy-start.6
  18.7 0.7 %copy-done.6 = s32[8]{0:T(128)S(1)} copy-done((s32[8]{0:T(128)S(1)}, s32[8]{0:T(128)}, u32[]{:S(2)}) %copy-start.6) | copy-done | bytes 56
  19.3 7.8 %attend.1 = (bf16[8,32,128]{2,1,0:T(8,128)(2,1)S(1)}, bf16[32,128]{1,0:T(8,128)(2,1)S(1)}, bf16[32,128]{1,0:T(8,128)(2,1)S(1)}, bf16[32,128]{1,0:T(8,128)(2,1)S(1)}) custom-call(s32[4,2]{1,0:T(4,128)S(1)} %copy-done.4, s32[8,8]{1,0:T(8,128)S(1)} %copy-done.5, s32[8]{0:T(128)S(1)} %copy-done.6, bf16[8,32,128]{2,1,0:T(8,128)(2,1)S(1)} %bitcast.16, ...), custom_call_target="tpu_custom_call" | custom-call | tf_op jit(solution)/shard_map/attend/pallas_call | solution.py:234
  27.1 0.0 copy-start.3
  27.1 0.6 %copy-done.3 = bf16[8,32,128]{2,1,0:T(8,128)(2,1)} copy-done((bf16[8,32,128]{2,1,0:T(8,128)(2,1)}, bf16[8,32,128]{2,1,0:T(8,128)(2,1)S(1)}, u32[]{:S(2)}) %copy-start.3) | copy-done | bytes 65560
  27.7 3.1 %collective-permute-start.3 = (bf16[32,128]{1,0:T(8,128)(2,1)S(1)}, bf16[32,128]{1,0:T(8,128)(2,1)S(1)}, u32[]{:S(2)}, u32[]{:S(2)}) collective-permute-start(bf16[32,128]{1,0:T(8,128)(2,1)S(1)} %get-tuple-element.16), channel_id=1, source_target_pairs={{0,12},{4,0},{8,4},{12,8},{1,13},{5,1},{9,5},{13,9},{2,14},{6,2},{... | collective-permute-start | bytes 24584 | tf_op jit(solution)/shard_map/ppermute | solution.py:259
  30.9 0.0 collective-permute-start.4
  30.9 0.6 %collective-permute-start.5 = (bf16[32,128]{1,0:T(8,128)(2,1)S(1)}, bf16[32,128]{1,0:T(8,128)(2,1)S(1)}, u32[]{:S(2)}, u32[]{:S(2)}) collective-permute-start(bf16[32,128]{1,0:T(8,128)(2,1)S(1)} %get-tuple-element.18), channel_id=1, source_target_pairs={{0,4},{4,8},{8,12},{12,0},{1,5},{5,9},{9,13},{13,1},{2,6},{6,10},{... | collective-permute-start | bytes 24584 | tf_op jit(solution)/shard_map/ppermute | solution.py:259
  31.5 0.8 %collective-permute-done.3.refs_0_ = bf16[32,128]{1,0:T(8,128)(2,1)S(1)} collective-permute-done((bf16[32,128]{1,0:T(8,128)(2,1)S(1)}, bf16[32,128]{1,0:T(8,128)(2,1)S(1)}, u32[]{:S(2)}, u32[]{:S(2)}) %collective-permute-start.3) | collective-permute-done | bytes 8224 | tf_op jit(solution)/shard_map/ppermute | solution.py:259
  32.3 0.0 copy-start.7
  32.3 3.2 %collective-permute-done.4.refs_1_ = bf16[32,128]{1,0:T(8,128)(2,1)S(1)} collective-permute-done((bf16[32,128]{1,0:T(8,128)(2,1)S(1)}, bf16[32,128]{1,0:T(8,128)(2,1)S(1)}, u32[]{:S(2)}, u32[]{:S(2)}) %collective-permute-start.4) | collective-permute-done | bytes 8224 | tf_op jit(solution)/shard_map/ppermute | solution.py:259
  35.4 0.0 copy-start.8
  35.4 0.9 %collective-permute-done.5.refs_2_ = bf16[32,128]{1,0:T(8,128)(2,1)S(1)} collective-permute-done((bf16[32,128]{1,0:T(8,128)(2,1)S(1)}, bf16[32,128]{1,0:T(8,128)(2,1)S(1)}, u32[]{:S(2)}, u32[]{:S(2)}) %collective-permute-start.5) | collective-permute-done | bytes 8224 | tf_op jit(solution)/shard_map/ppermute | solution.py:259
  36.3 0.0 copy-start.9
  36.3 0.0 copy-done.7
  36.3 0.0 copy-done.8
  36.3 0.6 %copy-done.9 = bf16[32,128]{1,0:T(8,128)(2,1)} copy-done((bf16[32,128]{1,0:T(8,128)(2,1)}, bf16[32,128]{1,0:T(8,128)(2,1)S(1)}, u32[]{:S(2)}) %copy-start.9) | copy-done | bytes 8216
  36.9 1.6 %place.1 = bf16[8,32,128]{2,1,0:T(8,128)(2,1)} custom-call(s32[4,2]{1,0:T(4,128)} %copy.11.moves, bf16[8,32,128]{2,1,0:T(8,128)(2,1)} %copy-done.3, bf16[32,128]{1,0:T(8,128)(2,1)} %copy-done.7, bf16[32,128]{1,0:T(8,128)(2,1)} %copy-done.8, bf16[32,128]{1,0:T(8,128)(2,1)} %copy-done.9), custom_call_target="tpu_custom_call" | custom-call | tf_op jit(solution)/shard_map/place/pallas_call | solution.py:260
Async XLA Ops:
  2.9 7.0 %collective-permute-start = (bf16[40,128]{1,0:T(8,128)(2,1)}, bf16[40,128]{1,0:T(8,128)(2,1)S(1)}, u32[]{:S(2)}, u32[]{:S(2)}) collective-permute-start(bf16[40,128]{1,0:T(8,128)(2,1)} %get-tuple-element.12), channel_id=1, source_target_pairs={{0,4},{4,8},{8,12},{12,0},{1,5},{5,9},{9,13},{13,1},{2,6},{6,10},{... | collective-permute-start | bytes 30728 | tf_op jit(solution)/shard_map/ppermute | solution.py:233
  5.9 4.9 %collective-permute-start.1 = (bf16[40,128]{1,0:T(8,128)(2,1)}, bf16[40,128]{1,0:T(8,128)(2,1)S(1)}, u32[]{:S(2)}, u32[]{:S(2)}) collective-permute-start(bf16[40,128]{1,0:T(8,128)(2,1)} %get-tuple-element.13), channel_id=1, source_target_pairs={{0,8},{4,12},{8,0},{12,4},{1,9},{5,13},{9,1},{13,5},{2,10},{6,14},... | collective-permute-start | bytes 30728 | tf_op jit(solution)/shard_map/ppermute | solution.py:233
  8.5 3.9 %collective-permute-start.2 = (bf16[40,128]{1,0:T(8,128)(2,1)}, bf16[40,128]{1,0:T(8,128)(2,1)S(1)}, u32[]{:S(2)}, u32[]{:S(2)}) collective-permute-start(bf16[40,128]{1,0:T(8,128)(2,1)} %get-tuple-element.14), channel_id=1, source_target_pairs={{0,12},{4,0},{8,4},{12,8},{1,13},{5,1},{9,5},{13,9},{2,14},{6,2},{... | collective-permute-start | bytes 30728 | tf_op jit(solution)/shard_map/ppermute | solution.py:233
  12.4 3.4 %copy-start = (bf16[16,2,512,256]{3,2,1,0:T(8,128)(2,1)S(1)}, bf16[16,2,512,256]{3,2,1,0:T(8,128)(2,1)}, u32[]{:S(2)}) copy-start(bf16[16,2,512,256]{3,2,1,0:T(8,128)(2,1)} %pool.1) | copy-start | bytes 25165828
  15.8 0.8 %copy-start.1 = (bf16[8,2,2048]{2,1,0:T(2,128)(2,1)S(1)}, bf16[8,2,2048]{2,1,0:T(2,128)(2,1)}, u32[]{:S(2)}) copy-start(bf16[8,2,2048]{2,1,0:T(2,128)(2,1)} %param.9) | copy-start | bytes 196612
  16.6 0.7 %copy-start.2 = (bf16[8,2,2,256]{3,2,1,0:T(2,128)(2,1)S(1)}, bf16[8,2,2,256]{3,2,1,0:T(2,128)(2,1)}, u32[]{:S(2)}) copy-start(bf16[8,2,2,256]{3,2,1,0:T(2,128)(2,1)} %param.10) | copy-start | bytes 49156
  17.3 0.7 %copy-start.4 = (s32[4,2]{1,0:T(4,128)S(1)}, s32[4,2]{1,0:T(4,128)}, u32[]{:S(2)}) copy-start(s32[4,2]{1,0:T(4,128)} %copy.11.moves) | copy-start | bytes 100
  18.0 0.7 %copy-start.5 = (s32[8,8]{1,0:T(8,128)S(1)}, s32[8,8]{1,0:T(8,128)}, u32[]{:S(2)}) copy-start(s32[8,8]{1,0:T(8,128)} %page_table.1) | copy-start | bytes 772
  18.6 0.7 %copy-start.6 = (s32[8]{0:T(128)S(1)}, s32[8]{0:T(128)}, u32[]{:S(2)}) copy-start(s32[8]{0:T(128)} %lengths.1) | copy-start | bytes 100
  27.1 0.6 %copy-start.3 = (bf16[8,32,128]{2,1,0:T(8,128)(2,1)}, bf16[8,32,128]{2,1,0:T(8,128)(2,1)S(1)}, u32[]{:S(2)}) copy-start(bf16[8,32,128]{2,1,0:T(8,128)(2,1)S(1)} %get-tuple-element.15.local) | copy-start | bytes 196612
  27.7 4.5 %collective-permute-start.3 = (bf16[32,128]{1,0:T(8,128)(2,1)S(1)}, bf16[32,128]{1,0:T(8,128)(2,1)S(1)}, u32[]{:S(2)}, u32[]{:S(2)}) collective-permute-start(bf16[32,128]{1,0:T(8,128)(2,1)S(1)} %get-tuple-element.16), channel_id=1, source_target_pairs={{0,12},{4,0},{8,4},{12,8},{1,13},{5,1},{9,5},{13,9},{2,14},{6,2},{... | collective-permute-start | bytes 24584 | tf_op jit(solution)/shard_map/ppermute | solution.py:259
  30.9 4.5 %collective-permute-start.4 = (bf16[32,128]{1,0:T(8,128)(2,1)S(1)}, bf16[32,128]{1,0:T(8,128)(2,1)S(1)}, u32[]{:S(2)}, u32[]{:S(2)}) collective-permute-start(bf16[32,128]{1,0:T(8,128)(2,1)S(1)} %get-tuple-element.17), channel_id=1, source_target_pairs={{0,8},{4,12},{8,0},{12,4},{1,9},{5,13},{9,1},{13,5},{2,10},{6,14},... | collective-permute-start | bytes 24584 | tf_op jit(solution)/shard_map/ppermute | solution.py:259
  30.9 5.4 %collective-permute-start.5 = (bf16[32,128]{1,0:T(8,128)(2,1)S(1)}, bf16[32,128]{1,0:T(8,128)(2,1)S(1)}, u32[]{:S(2)}, u32[]{:S(2)}) collective-permute-start(bf16[32,128]{1,0:T(8,128)(2,1)S(1)} %get-tuple-element.18), channel_id=1, source_target_pairs={{0,4},{4,8},{8,12},{12,0},{1,5},{5,9},{9,13},{13,1},{2,6},{6,10},{... | collective-permute-start | bytes 24584 | tf_op jit(solution)/shard_map/ppermute | solution.py:259
  32.3 4.1 %copy-start.7 = (bf16[32,128]{1,0:T(8,128)(2,1)}, bf16[32,128]{1,0:T(8,128)(2,1)S(1)}, u32[]{:S(2)}) copy-start(bf16[32,128]{1,0:T(8,128)(2,1)S(1)} %collective-permute-done.3.refs_0_) | copy-start | bytes 24580
  35.4 0.9 %copy-start.8 = (bf16[32,128]{1,0:T(8,128)(2,1)}, bf16[32,128]{1,0:T(8,128)(2,1)S(1)}, u32[]{:S(2)}) copy-start(bf16[32,128]{1,0:T(8,128)(2,1)S(1)} %collective-permute-done.4.refs_1_) | copy-start | bytes 24580
  36.3 0.6 %copy-start.9 = (bf16[32,128]{1,0:T(8,128)(2,1)}, bf16[32,128]{1,0:T(8,128)(2,1)S(1)}, u32[]{:S(2)}) copy-start(bf16[32,128]{1,0:T(8,128)(2,1)S(1)} %collective-permute-done.5.refs_2_) | copy-start | bytes 24580

commit v2 on v1

--- a/solution.py
+++ b/solution.py
@@ -12,48 +12,55 @@
 NEG = -1e30
 SMEM = pltpu.SMEM
 VMEM = pltpu.VMEM
-ANY = pl.ANY
+HBM = pltpu.HBM
 
 
 def find_moves(moves, rows_inst, n, me, hidden, cache):
-    for d in range(n):
+    for d in range(n + 1):
         if hidden is not None:
             hidden[d] = -1
         if cache is not None:
             cache[d] = -1
 
     def step(m, carry):
-        cache_slot = moves[m, 0]
-        hidden_slot = moves[m, 1]
+        cache_slot = moves[0, m]
+        hidden_slot = moves[1, m]
         from_inst = cache_slot // rows_inst
         to_inst = hidden_slot // rows_inst
-        shift = lax.rem(from_inst - to_inst + n, n)
         if hidden is not None:
-            hidden[jnp.where(to_inst == me, shift, 0)] = lax.rem(hidden_slot, rows_inst)
+            hidden[jnp.where(to_inst == me, from_inst, n)] = lax.rem(hidden_slot, rows_inst)
         if cache is not None:
-            cache[jnp.where(from_inst == me, shift, 0)] = lax.rem(cache_slot, rows_inst)
+            cache[jnp.where(from_inst == me, to_inst, n)] = lax.rem(cache_slot, rows_inst)
         return carry
 
-    lax.fori_loop(0, moves.shape[0], step, 0)
-
-
-def pack_kernel(n, moves, q, kv, *refs):
-    outs, hidden = refs[: n - 1], refs[n - 1]
-    rows_inst = q.shape[0]
-    heads = q.shape[1]
+    lax.fori_loop(0, moves.shape[1], step, 0)
+
+
+def pack_kernel(n, moves_hbm, q_hbm, kv_hbm, out, hidden, moves, q, kv, sems):
+    copies = [
+        pltpu.make_async_copy(moves_hbm, moves, sems.at[0]),
+        pltpu.make_async_copy(q_hbm, q, sems.at[1]),
+        pltpu.make_async_copy(kv_hbm, kv, sems.at[2]),
+    ]
+    for c in copies:
+        c.start()
+    rows_inst, heads, _ = q.shape
     me = lax.axis_index("inst")
+    copies[0].wait()
     find_moves(moves, rows_inst, n, me, hidden, None)
-    for d in range(1, n):
+    copies[1].wait()
+    copies[2].wait()
+    for d in range(n):
         slot = jnp.maximum(hidden[d], 0)
-        outs[d - 1][0:heads, :] = q[slot]
-        outs[d - 1][heads:, :] = kv[slot]
-
-
-def attend_kernel(n, moves, page_table, lengths, q, kv, pool, *refs):
-    recv = refs[: n - 1]
-    out = refs[n - 1]
-    back = refs[n : 2 * n - 1]
-    (cache, owner, limit, vacant, buf, qbd, fk, scores, part_max, top, part_sum, acc, sems) = refs[2 * n - 1 :]
+        out[d, 0:heads, :] = q[slot]
+        out[d, heads:, :] = kv[slot]
+
+
+def attend_kernel(n, moves_hbm, page_hbm, length_hbm, q_hbm, kv_hbm, pool, recv, local, back, *refs):
+    (
+        moves, page_table, lengths, cache, owner, limit, vacant,
+        q, kv, out, buf, qbd, fk, scores, part_max, top, part_sum, acc, small_sems, sems, out_sem,
+    ) = refs
     rows_inst, heads, hd = q.shape
     fresh_rows = kv.shape[1]
     slots, _, block, columns = pool.shape
@@ -64,12 +71,23 @@
     me = lax.axis_index("inst")
     scale = 1.0 / math.sqrt(hd)
 
+    small = [
+        pltpu.make_async_copy(src, dst, small_sems.at[i])
+        for i, (src, dst) in enumerate(
+            [(moves_hbm, moves), (page_hbm, page_table), (length_hbm, lengths), (q_hbm, q), (kv_hbm, kv)]
+        )
+    ]
+    for c in small:
+        c.start()
+
     def fetch(p, plane):
         return pltpu.make_async_copy(pool.at[p, plane], buf.at[p, plane], sems.at[p, plane])
 
     for plane in range(2):
         for p in range(slots):
             fetch(p, plane).start()
+    for c in small:
+        c.wait()
 
     find_moves(moves, rows_inst, n, me, None, cache)
     for p in range(slots + 1):
@@ -96,12 +114,12 @@
     for r in range(rows_inst):
         set_row(r, q[r], kv[r])
     set_row(rows_inst, q[0], kv[0])
-    for d in range(1, n):
+    for d in range(n):
 
         @pl.when(cache[d] >= 0)
         def _():
             slot = cache[d]
-            set_row(slot, recv[d - 1][0:heads, :], recv[d - 1][heads:, :])
+            set_row(slot, recv[d, 0:heads, :], recv[d, heads:, :])
             vacant[slot] = 1
 
     step_of = lax.broadcasted_iota(jnp.int32, (per, 1), 0) % steps
@@ -181,22 +199,28 @@
         value = acc[r] / total
         acc[r] = value
         out[r] = jnp.where(vacant[r] == 1, 0.0, value).astype(jnp.bfloat16)
-    for d in range(1, n):
-        back[d - 1][...] = acc[jnp.maximum(cache[d], 0)].astype(jnp.bfloat16)
-
-
-def place_kernel(n, moves, local, *refs):
-    back = refs[: n - 1]
-    out, hidden = refs[n - 1 :]
-    rows_inst = local.shape[0]
-    me = lax.axis_index("inst")
-    find_moves(moves, rows_inst, n, me, hidden, None)
-    out[...] = local[...]
-    for d in range(1, n):
+    write = pltpu.make_async_copy(out, local, out_sem)
+    write.start()
+    for d in range(n):
+        back[d] = acc[jnp.maximum(cache[d], 0)].astype(jnp.bfloat16)
+    write.wait()
+
+
+def place_kernel(n, hidden, local, back, out, sems):
+    def put(d):
+        return pltpu.make_async_copy(back.at[d], out.at[jnp.maximum(hidden[d], 0)], sems.at[d])
+
+    for d in range(n):
 
         @pl.when(hidden[d] >= 0)
         def _():
-            out[hidden[d]] = back[d - 1][...]
+            put(d).start()
+
+    for d in range(n):
+
+        @pl.when(hidden[d] >= 0)
+        def _():
+            put(d).wait()
 
 
 def body(kv_pool, page_table, lengths, queries, new_kv, moves):
@@ -208,40 +232,59 @@
     heads_all = width // HD
     heads = steps * heads_all
     fresh_rows = steps * groups * 2
+    pages = page_table.shape[1]
     bf16 = jnp.bfloat16
     f32 = jnp.float32
+    i32 = jnp.int32
     q = queries.reshape(rows_inst, steps, heads_all, HD).transpose(0, 2, 1, 3).reshape(rows_inst, heads, HD)
     kv = (
         new_kv.reshape(rows_inst, steps, 2, groups, HD)
         .transpose(0, 1, 3, 2, 4)
         .reshape(rows_inst, fresh_rows, HD)
     )
+    in_hbm = lambda x: pltpu.with_memory_space_constraint(x, HBM)
+    q, kv, kv_pool, page_table, lengths = map(in_hbm, (q, kv, kv_pool, page_table, lengths))
+    move_cols = in_hbm(moves.T)
     smem = pl.BlockSpec(memory_space=SMEM)
     vmem = pl.BlockSpec(memory_space=VMEM)
-    anyspace = pl.BlockSpec(memory_space=ANY)
-    forward = [[(i, (i + d) % n) for i in range(n)] for d in range(1, n)]
-    backward = [[(i, (i - d) % n) for i in range(n)] for d in range(1, n)]
-
-    packed = pl.pallas_call(
+    hbm = pl.BlockSpec(memory_space=HBM)
+
+    packed, hidden = pl.pallas_call(
         functools.partial(pack_kernel, n),
-        out_shape=[jax.ShapeDtypeStruct((heads + fresh_rows, HD), bf16)] * (n - 1),
-        in_specs=[smem, vmem, vmem],
-        out_specs=[vmem] * (n - 1),
-        scratch_shapes=[SMEM((n,), jnp.int32)],
+        out_shape=[
+            jax.ShapeDtypeStruct((n, heads + fresh_rows, HD), bf16),
+            SMEM((n + 1,), i32),
+        ],
+        in_specs=[hbm, hbm, hbm],
+        out_specs=[vmem, smem],
+        scratch_shapes=[
+            SMEM(move_cols.shape, i32),
+            VMEM(q.shape, bf16),
+            VMEM(kv.shape, bf16),
+            pltpu.SemaphoreType.DMA((3,)),
+        ],
         name="pack",
-    )(moves, q, kv)
-    received = [lax.ppermute(x, "inst", perm) for x, perm in zip(packed, forward)]
-    results = pl.pallas_call(
+    )(move_cols, q, kv)
+    received = lax.all_to_all(packed, "inst", 0, 0)
+    local, back = pl.pallas_call(
         functools.partial(attend_kernel, n),
-        out_shape=[jax.ShapeDtypeStruct((rows_inst, heads, HD), bf16)]
-        + [jax.ShapeDtypeStruct((heads, HD), bf16)] * (n - 1),
-        in_specs=[smem, smem, smem, vmem, vmem, anyspace] + [vmem] * (n - 1),
-        out_specs=[vmem] * n,
+        out_shape=[
+            jax.ShapeDtypeStruct((rows_inst, heads, HD), bf16),
+            jax.ShapeDtypeStruct((n, heads, HD), bf16),
+        ],
+        in_specs=[hbm] * 6 + [vmem],
+        out_specs=[hbm, vmem],
         scratch_shapes=[
-            SMEM((n,), jnp.int32),
-            SMEM((slots + 1,), jnp.int32),
-            SMEM((slots + 1,), jnp.int32),
-            SMEM((rows_inst,), jnp.int32),
+            SMEM(move_cols.shape, i32),
+            SMEM(page_table.shape, i32),
+            SMEM(lengths.shape, i32),
+            SMEM((n + 1,), i32),
+            SMEM((slots + 1,), i32),
+            SMEM((slots + 1,), i32),
+            SMEM((rows_inst,), i32),
+            VMEM(q.shape, bf16),
+            VMEM(kv.shape, bf16),
+            VMEM((rows_inst, heads, HD), bf16),
             VMEM((slots, 2, block, columns), bf16),
             VMEM((rows_inst + 1, heads, columns), bf16),
             VMEM((rows_inst + 1, fresh_rows, HD), f32),
@@ -250,21 +293,23 @@
             VMEM((rows_inst + 1, heads, HD), f32),
             VMEM((rows_inst + 1, heads, HD), f32),
             VMEM((rows_inst + 1, heads, HD), f32),
+            pltpu.SemaphoreType.DMA((5,)),
             pltpu.SemaphoreType.DMA((slots, 2)),
+            pltpu.SemaphoreType.DMA,
         ],
         compiler_params=pltpu.CompilerParams(vmem_limit_bytes=24 * 1024 * 1024),
         name="attend",
-    )(moves, page_table, lengths, q, kv, kv_pool, *received)
-    local, back = results[0], results[1:]
-    returned = [lax.ppermute(x, "inst", perm) for x, perm in zip(back, backward)]
+    )(move_cols, page_table, lengths, q, kv, kv_pool, received)
+    returned = lax.all_to_all(back, "inst", 0, 0)
     out = pl.pallas_call(
         functools.partial(place_kernel, n),
         out_shape=jax.ShapeDtypeStruct((rows_inst, heads, HD), bf16),
-        in_specs=[smem, vmem] + [vmem] * (n - 1),
-        out_specs=vmem,
-        scratch_shapes=[SMEM((n,), jnp.int32)],
+        in_specs=[smem, hbm, vmem],
+        out_specs=hbm,
+        scratch_shapes=[pltpu.SemaphoreType.DMA((n,))],
+        input_output_aliases={1: 0},
         name="place",
-    )(moves, local, *returned)
+    )(hidden, local, returned)
     return out.reshape(rows_inst, heads_all, steps, HD).transpose(0, 2, 1, 3).reshape(rows_inst, steps, width)
 
 

time: 39 us -> 33.7 us (0.86)
  blocking collectives: 0 us -> 20.7 us
  starting transfers between devices: 10.7 us -> 0 us
  local copies, waits for them, and re-layouts: 9.47 us -> 0 us
  waiting for transfers between devices: 7.41 us -> 0 us
  Pallas kernels: 11 us -> 12.6 us
    all_to_all x0 -> x2, blocking collectives: none -> 20.7 us  [the longest x1 12 us: body(): received = lax.all_to_all(packed, 'inst', 0, 0)]
    ppermute x6 -> x0, starting transfers between devices: 10.7 us -> none  [body(): lax.ppermute(x, 'inst', perm)]
    unnamed x21 -> x0, local copies, waits for them, and re-layouts: 9.47 us -> none
    ppermute x6 -> x0, waiting for transfers between devices: 7.41 us -> none  [body(): lax.ppermute(x, 'inst', perm)]
    pallas_call x1, Pallas kernels: 7.8 us -> 10.4 us  [body(): pl.pallas_call(functools.partial(attend_kernel, n), out_shape=[jax.ShapeD...]
    pallas_call x1, Pallas kernels: 1.61 us -> 0.79 us  [body(): pl.pallas_call(functools.partial(place_kernel, n), out_shape=jax.ShapeDty...]
  transfers between devices with their start and end apart: 6 -> 0, of which waited for: 5 -> 0; matrix products, arithmetic and copies ran while one was open for 0% -> 0% of each run, Pallas kernels for 0% -> 0%
where the time goes in v2:
time: 33.7 us; the launch traced here: 33.4 us
  blocking collectives  20.7 us (61%)
  Pallas kernels  12.6 us (37%)
    all_to_all x1, blocking collectives, body(): received = lax.all_to_all(packed, 'inst', 0, 0)  12 us
    pallas_call x1, Pallas kernels, body(): pl.pallas_call(functools.partial(attend_kernel, n), out_shape=[jax.ShapeD...  10.4 us
    all_to_all x1, blocking collectives, body(): returned = lax.all_to_all(back, 'inst', 0, 0)  8.69 us
    pallas_call x1, Pallas kernels, body(): pl.pallas_call(functools.partial(pack_kernel, n), out_shape=[jax.ShapeDty...  1.49 us
    pallas_call x1, Pallas kernels, body(): pl.pallas_call(functools.partial(place_kernel, n), out_shape=jax.ShapeDty...  0.79 us

profile of v2, /device:TPU:0, one launch (start us, length us, event | category | flops | bytes accessed | tf_op | source)
XLA Modules:
  0.0 33.4 jit_solution(81800459159980879)
XLA Ops:
  0.0 1.5 %pack.1 = (bf16[4,40,128]{2,1,0:T(8,128)(2,1)}, s32[5]{0:T(128)S(4)}) custom-call(s32[2,4]{1,0:T(2,128)} %bitcast.20, bf16[8,32,128]{2,1,0:T(8,128)(2,1)} %bitcast.16, bf16[8,8,128]{2,1,0:T(8,128)(2,1)} %bitcast.18), custom_call_target="tpu_custom_call" | custom-call | tf_op jit(solution)/shard_map/pack/pallas_call | solution.py:252
  1.5 12.0 %all_to_all.10.recv = bf16[4,40,128]{2,1,0:T(8,128)(2,1)S(1)} all-to-all(bf16[4,40,128]{2,1,0:T(8,128)(2,1)} %get-tuple-element.10), channel_id=1, replica_groups=mesh['groups'=2,'inst'=4,'tp'=4] {'inst'}, dimensions={0} | all-to-all | bytes 81920 | tf_op jit(solution)/shard_map/all_to_all | solution.py:268
  13.5 10.4 %attend.1 = (bf16[8,32,128]{2,1,0:T(8,128)(2,1)}, bf16[4,32,128]{2,1,0:T(8,128)(2,1)S(1)}) custom-call(s32[2,4]{1,0:T(2,128)} %bitcast.21, s32[8,8]{1,0:T(8,128)} %page_hbm.1, s32[8]{0:T(128)} %length_hbm.1, bf16[8,32,128]{2,1,0:T(8,128)(2,1)} %bitcast.17, bf16[8,8,128]{2,1,0:T(8,128)(2,1)} %bitcast.19, bf16[16,2,512,256]{3,2,1,0:T(8,128)(2,1)} %pool.1, ...), custom_call_target="tpu_custom_call" | custom-call | tf_op jit(solution)/shard_map/attend/pallas_call | solution.py:269
  23.9 8.7 %all_to_all.11.back = bf16[4,32,128]{2,1,0:T(8,128)(2,1)} all-to-all(bf16[4,32,128]{2,1,0:T(8,128)(2,1)S(1)} %get-tuple-element.12), channel_id=1, replica_groups=mesh['groups'=2,'inst'=4,'tp'=4] {'inst'}, dimensions={0} | all-to-all | bytes 65536 | tf_op jit(solution)/shard_map/all_to_all | solution.py:303
  32.6 0.8 %place.1 = bf16[8,32,128]{2,1,0:T(8,128)(2,1)} custom-call(s32[5]{0:T(128)S(4)} %get-tuple-element.9.hidden, bf16[8,32,128]{2,1,0:T(8,128)(2,1)} %get-tuple-element.11.local, bf16[4,32,128]{2,1,0:T(8,128)(2,1)} %all_to_all.11.back), custom_call_target="tpu_custom_call", output_to_operand_aliasing={{}: (1, {})} | custom-call | tf_op jit(solution)/shard_map/place/pallas_call | solution.py:304

commit v3 on v2

--- a/solution.py
+++ b/solution.py
@@ -15,28 +15,20 @@
 HBM = pltpu.HBM
 
 
-def find_moves(moves, rows_inst, n, me, hidden, cache):
-    for d in range(n + 1):
-        if hidden is not None:
-            hidden[d] = -1
-        if cache is not None:
-            cache[d] = -1
-
-    def step(m, carry):
-        cache_slot = moves[0, m]
-        hidden_slot = moves[1, m]
-        from_inst = cache_slot // rows_inst
-        to_inst = hidden_slot // rows_inst
-        if hidden is not None:
-            hidden[jnp.where(to_inst == me, from_inst, n)] = lax.rem(hidden_slot, rows_inst)
-        if cache is not None:
-            cache[jnp.where(from_inst == me, to_inst, n)] = lax.rem(cache_slot, rows_inst)
-        return carry
-
-    lax.fori_loop(0, moves.shape[1], step, 0)
-
-
-def pack_kernel(n, moves_hbm, q_hbm, kv_hbm, out, hidden, moves, q, kv, sems):
+def partner(n):
+    if n & (n - 1) == 0:
+        swap = lambda d: [(i, i ^ d) for i in range(n)]
+        return (lambda a, b: a ^ b), swap, swap
+    return (
+        (lambda a, b: lax.rem(a - b + n, n)),
+        lambda d: [(i, (i + d) % n) for i in range(n)],
+        lambda d: [(i, (i - d) % n) for i in range(n)],
+    )
+
+
+def pack_kernel(n, moves_hbm, q_hbm, kv_hbm, *refs):
+    outs = refs[: n - 1]
+    hidden, cache, moves, q, kv, sems = refs[n - 1 :]
     copies = [
         pltpu.make_async_copy(moves_hbm, moves, sems.at[0]),
         pltpu.make_async_copy(q_hbm, q, sems.at[1]),
@@ -46,21 +38,37 @@
         c.start()
     rows_inst, heads, _ = q.shape
     me = lax.axis_index("inst")
+    index_of = partner(n)[0]
+    for d in range(n):
+        hidden[d] = -1
+        cache[d] = -1
     copies[0].wait()
-    find_moves(moves, rows_inst, n, me, hidden, None)
+
+    def step(m, carry):
+        cache_slot = moves[0, m]
+        hidden_slot = moves[1, m]
+        from_inst = cache_slot // rows_inst
+        to_inst = hidden_slot // rows_inst
+        index = index_of(from_inst, to_inst)
+        hidden[jnp.where(to_inst == me, index, 0)] = lax.rem(hidden_slot, rows_inst)
+        cache[jnp.where(from_inst == me, index, 0)] = lax.rem(cache_slot, rows_inst)
+        return carry
+
+    lax.fori_loop(0, moves.shape[1], step, 0, unroll=moves.shape[1] <= 8)
     copies[1].wait()
     copies[2].wait()
-    for d in range(n):
+    for d in range(1, n):
         slot = jnp.maximum(hidden[d], 0)
-        out[d, 0:heads, :] = q[slot]
-        out[d, heads:, :] = kv[slot]
-
-
-def attend_kernel(n, moves_hbm, page_hbm, length_hbm, q_hbm, kv_hbm, pool, recv, local, back, *refs):
+        outs[d - 1][0:heads, :] = q[slot]
+        outs[d - 1][heads:, :] = kv[slot]
+
+
+def attend_kernel(n, chunk, cache, page_hbm, length_hbm, q_hbm, kv_hbm, pool, *refs):
+    recv, local, back = refs[: n - 1], refs[n - 1], refs[n : 2 * n - 1]
     (
-        moves, page_table, lengths, cache, owner, limit, vacant,
+        page_table, lengths, owner, limit, vacant,
         q, kv, out, buf, qbd, fk, scores, part_max, top, part_sum, acc, small_sems, sems, out_sem,
-    ) = refs
+    ) = refs[2 * n - 1 :]
     rows_inst, heads, hd = q.shape
     fresh_rows = kv.shape[1]
     slots, _, block, columns = pool.shape
@@ -68,28 +76,32 @@
     steps = fresh_rows // (2 * groups)
     per = heads // groups
     pages = page_table.shape[1]
-    me = lax.axis_index("inst")
     scale = 1.0 / math.sqrt(hd)
 
     small = [
         pltpu.make_async_copy(src, dst, small_sems.at[i])
         for i, (src, dst) in enumerate(
-            [(moves_hbm, moves), (page_hbm, page_table), (length_hbm, lengths), (q_hbm, q), (kv_hbm, kv)]
+            [(page_hbm, page_table), (length_hbm, lengths), (q_hbm, q), (kv_hbm, kv)]
         )
     ]
     for c in small:
         c.start()
 
-    def fetch(p, plane):
-        return pltpu.make_async_copy(pool.at[p, plane], buf.at[p, plane], sems.at[p, plane])
+    def fetch(k, plane):
+        part = pl.ds(k * chunk, chunk)
+        return pltpu.make_async_copy(pool.at[part, plane], buf.at[part, plane], sems.at[k, plane])
+
+    def arrived(p, plane):
+        if p % (slots // 2) == 0:
+            for k in range(p // chunk, (p + slots // 2) // chunk):
+                fetch(k, plane).wait()
 
     for plane in range(2):
-        for p in range(slots):
-            fetch(p, plane).start()
+        for k in range(slots // chunk):
+            fetch(k, plane).start()
     for c in small:
         c.wait()
 
-    find_moves(moves, rows_inst, n, me, None, cache)
     for p in range(slots + 1):
         owner[p] = rows_inst
         limit[p] = 0
@@ -114,12 +126,12 @@
     for r in range(rows_inst):
         set_row(r, q[r], kv[r])
     set_row(rows_inst, q[0], kv[0])
-    for d in range(n):
+    for d in range(1, n):
 
         @pl.when(cache[d] >= 0)
         def _():
             slot = cache[d]
-            set_row(slot, recv[d, 0:heads, :], recv[d, heads:, :])
+            set_row(slot, recv[d - 1][0:heads, :], recv[d - 1][heads:, :])
             vacant[slot] = 1
 
     step_of = lax.broadcasted_iota(jnp.int32, (per, 1), 0) % steps
@@ -143,7 +155,7 @@
 
     lane = lax.broadcasted_iota(jnp.int32, (heads, block), 1)
     for p in range(slots):
-        fetch(p, 0).wait()
+        arrived(p, 0)
         r = owner[p]
         s = lax.dot_general(
             qbd[r], buf[p, 0], (((1,), (1,)), ((), ())), preferred_element_type=jnp.float32
@@ -176,7 +188,7 @@
     acc[rows_inst] = jnp.zeros((heads, hd), jnp.float32)
 
     for p in range(slots):
-        fetch(p, 1).wait()
+        arrived(p, 1)
         r = owner[p]
         m = top[r]
         pieces = []
@@ -201,22 +213,24 @@
         out[r] = jnp.where(vacant[r] == 1, 0.0, value).astype(jnp.bfloat16)
     write = pltpu.make_async_copy(out, local, out_sem)
     write.start()
-    for d in range(n):
-        back[d] = acc[jnp.maximum(cache[d], 0)].astype(jnp.bfloat16)
+    for d in range(1, n):
+        back[d - 1][...] = acc[jnp.maximum(cache[d], 0)].astype(jnp.bfloat16)
     write.wait()
 
 
-def place_kernel(n, hidden, local, back, out, sems):
+def place_kernel(n, hidden, local, *refs):
+    back, out, sems = refs[: n - 1], refs[n - 1], refs[n]
+
     def put(d):
-        return pltpu.make_async_copy(back.at[d], out.at[jnp.maximum(hidden[d], 0)], sems.at[d])
-
-    for d in range(n):
+        return pltpu.make_async_copy(back[d - 1], out.at[jnp.maximum(hidden[d], 0)], sems.at[d])
+
+    for d in range(1, n):
 
         @pl.when(hidden[d] >= 0)
         def _():
             put(d).start()
 
-    for d in range(n):
+    for d in range(1, n):
 
         @pl.when(hidden[d] >= 0)
         def _():
@@ -249,14 +263,15 @@
     vmem = pl.BlockSpec(memory_space=VMEM)
     hbm = pl.BlockSpec(memory_space=HBM)
 
-    packed, hidden = pl.pallas_call(
+    _, forward, backward = partner(n)
+    chunk = math.gcd(slots, 4)
+
+    *packed, hidden, cache = pl.pallas_call(
         functools.partial(pack_kernel, n),
-        out_shape=[
-            jax.ShapeDtypeStruct((n, heads + fresh_rows, HD), bf16),
-            SMEM((n + 1,), i32),
-        ],
+        out_shape=[jax.ShapeDtypeStruct((heads + fresh_rows, HD), bf16)] * (n - 1)
+        + [SMEM((n,), i32), SMEM((n,), i32)],
         in_specs=[hbm, hbm, hbm],
-        out_specs=[vmem, smem],
+        out_specs=[vmem] * (n - 1) + [smem, smem],
         scratch_shapes=[
             SMEM(move_cols.shape, i32),
             VMEM(q.shape, bf16),
@@ -265,20 +280,16 @@
         ],
         name="pack",
     )(move_cols, q, kv)
-    received = lax.all_to_all(packed, "inst", 0, 0)
-    local, back = pl.pallas_call(
-        functools.partial(attend_kernel, n),
-        out_shape=[
-            jax.ShapeDtypeStruct((rows_inst, heads, HD), bf16),
-            jax.ShapeDtypeStruct((n, heads, HD), bf16),
-        ],
-        in_specs=[hbm] * 6 + [vmem],
-        out_specs=[hbm, vmem],
+    received = [lax.ppermute(x, "inst", forward(d + 1)) for d, x in enumerate(packed)]
+    local, *back = pl.pallas_call(
+        functools.partial(attend_kernel, n, chunk),
+        out_shape=[jax.ShapeDtypeStruct((rows_inst, heads, HD), bf16)]
+        + [jax.ShapeDtypeStruct((heads, HD), bf16)] * (n - 1),
+        in_specs=[smem] + [hbm] * 5 + [vmem] * (n - 1),
+        out_specs=[hbm] + [vmem] * (n - 1),
         scratch_shapes=[
-            SMEM(move_cols.shape, i32),
             SMEM(page_table.shape, i32),
             SMEM(lengths.shape, i32),
-            SMEM((n + 1,), i32),
             SMEM((slots + 1,), i32),
             SMEM((slots + 1,), i32),
             SMEM((rows_inst,), i32),
@@ -293,23 +304,23 @@
             VMEM((rows_inst + 1, heads, HD), f32),
             VMEM((rows_inst + 1, heads, HD), f32),
             VMEM((rows_inst + 1, heads, HD), f32),
-            pltpu.SemaphoreType.DMA((5,)),
-            pltpu.SemaphoreType.DMA((slots, 2)),
+            pltpu.SemaphoreType.DMA((4,)),
+            pltpu.SemaphoreType.DMA((slots // chunk, 2)),
             pltpu.SemaphoreType.DMA,
         ],
         compiler_params=pltpu.CompilerParams(vmem_limit_bytes=24 * 1024 * 1024),
         name="attend",
-    )(move_cols, page_table, lengths, q, kv, kv_pool, received)
-    returned = lax.all_to_all(back, "inst", 0, 0)
+    )(cache, page_table, lengths, q, kv, kv_pool, *received)
+    returned = [lax.ppermute(x, "inst", backward(d + 1)) for d, x in enumerate(back)]
     out = pl.pallas_call(
         functools.partial(place_kernel, n),
         out_shape=jax.ShapeDtypeStruct((rows_inst, heads, HD), bf16),
-        in_specs=[smem, hbm, vmem],
+        in_specs=[smem, hbm] + [vmem] * (n - 1),
         out_specs=hbm,
         scratch_shapes=[pltpu.SemaphoreType.DMA((n,))],
         input_output_aliases={1: 0},
         name="place",
-    )(hidden, local, returned)
+    )(hidden, local, *returned)
     return out.reshape(rows_inst, heads_all, steps, HD).transpose(0, 2, 1, 3).reshape(rows_inst, steps, width)
 
 

time: 33.7 us -> 27.6 us (0.82)
  blocking collectives: 20.7 us -> 0 us
  starting transfers between devices: 0 us -> 10.1 us
  waiting for transfers between devices: 0 us -> 7.4 us
  Pallas kernels: 12.6 us -> 8.9 us
  local copies, waits for them, and re-layouts: 0 us -> 0.6 us
    all_to_all x2 -> x0, blocking collectives: 20.7 us -> none  [the longest x1 12 us: body(): received = lax.all_to_all(packed, 'inst', 0, 0)]
    ppermute x0 -> x6, starting transfers between devices: none -> 10.1 us  [the longest x3 5.68 us: body(): lax.ppermute(x, 'inst', forward(d + 1))]
    ppermute x0 -> x6, waiting for transfers between devices: none -> 7.4 us  [the longest x3 5.68 us: body(): lax.ppermute(x, 'inst', forward(d + 1))]
    pallas_call x1, Pallas kernels: 10.4 us -> 6.67 us  [body(): pl.pallas_call(functools.partial(attend_kernel, n, chunk), out_shape=[jax...]
    unnamed x0 -> x6, local copies, waits for them, and re-layouts: none -> 0.6 us
  transfers between devices with their start and end apart: 0 -> 6, of which waited for: 0 -> 4; matrix products, arithmetic and copies ran while one was open for 0% -> 0% of each run, Pallas kernels for 0% -> 0%
where the time goes in v3:
time: 27.6 us; the launch traced here: 27.1 us
  starting transfers between devices  10.1 us (37%)
  Pallas kernels  8.9 us (32%)
  waiting for transfers between devices  7.4 us (27%)
  local copies, waits for them, and re-layouts  0.6 us (2%)
    pallas_call x1, Pallas kernels, body(): pl.pallas_call(functools.partial(attend_kernel, n, chunk), out_shape=[jax...  6.67 us
    ppermute x3, starting transfers between devices, body(): lax.ppermute(x, 'inst', forward(d + 1))  5.68 us
    ppermute x3, waiting for transfers between devices, body(): lax.ppermute(x, 'inst', forward(d + 1))  5.68 us
    ppermute x3, starting transfers between devices, body(): lax.ppermute(x, 'inst', backward(d + 1))  4.44 us
    ppermute x3, waiting for transfers between devices, body(): lax.ppermute(x, 'inst', backward(d + 1))  1.72 us
    pallas_call x1, Pallas kernels, body(): pl.pallas_call(functools.partial(pack_kernel, n), out_shape=[jax.ShapeDty...  1.47 us
    pallas_call x1, Pallas kernels, body(): pl.pallas_call(functools.partial(place_kernel, n), out_shape=jax.ShapeDty...  0.77 us
    unnamed x6, local copies, waits for them, and re-layouts  0.6 us
  transfers between devices with their start and end apart: 6, of which 4 were waited for; matrix products, arithmetic and copies ran while one was open for 0% of the time, Pallas kernels for 0%

profile of v3, /device:TPU:0, one launch (start us, length us, event | category | flops | bytes accessed | tf_op | source)
XLA Modules:
  0.0 27.1 jit_solution(3808105250993801517)
XLA Ops:
  0.0 1.5 %pack.1 = (bf16[40,128]{1,0:T(8,128)(2,1)}, bf16[40,128]{1,0:T(8,128)(2,1)}, bf16[40,128]{1,0:T(8,128)(2,1)}, s32[4]{0:T(128)S(4)}, s32[4]{0:T(128)S(4)}) custom-call(s32[2,4]{1,0:T(2,128)} %bitcast.20, bf16[8,32,128]{2,1,0:T(8,128)(2,1)} %bitcast.16, bf16[8,8,128]{2,1,0:T(8,128)(2,1)} %bitcast.18), custom_call_target="tpu_custom_call" | custom-call | tf_op jit(solution)/shard_map/pack/pallas_call | solution.py:269
  1.5 3.1 %collective-permute-start = (bf16[40,128]{1,0:T(8,128)(2,1)}, bf16[40,128]{1,0:T(8,128)(2,1)S(1)}, u32[]{:S(2)}, u32[]{:S(2)}) collective-permute-start(bf16[40,128]{1,0:T(8,128)(2,1)} %get-tuple-element.16), channel_id=1, source_target_pairs={{0,4},{4,0},{8,12},{12,8},{1,5},{5,1},{9,13},{13,9},{2,6},{6,2},{1... | collective-permute-start | bytes 30728 | tf_op jit(solution)/shard_map/ppermute | solution.py:283
  4.6 2.6 %collective-permute-start.1 = (bf16[40,128]{1,0:T(8,128)(2,1)}, bf16[40,128]{1,0:T(8,128)(2,1)S(1)}, u32[]{:S(2)}, u32[]{:S(2)}) collective-permute-start(bf16[40,128]{1,0:T(8,128)(2,1)} %get-tuple-element.17), channel_id=1, source_target_pairs={{0,8},{4,12},{8,0},{12,4},{1,9},{5,13},{9,1},{13,5},{2,10},{6,14},... | collective-permute-start | bytes 30728 | tf_op jit(solution)/shard_map/ppermute | solution.py:283
  7.2 0.0 collective-permute-start.2
  7.2 0.0 collective-permute-done.refs_0_
  7.2 2.2 %collective-permute-done.1.refs_1_ = bf16[40,128]{1,0:T(8,128)(2,1)S(1)} collective-permute-done((bf16[40,128]{1,0:T(8,128)(2,1)}, bf16[40,128]{1,0:T(8,128)(2,1)S(1)}, u32[]{:S(2)}, u32[]{:S(2)}) %collective-permute-start.1) | collective-permute-done | bytes 10272 | tf_op jit(solution)/shard_map/ppermute | solution.py:283
  9.4 3.5 %collective-permute-done.2.refs_2_ = bf16[40,128]{1,0:T(8,128)(2,1)S(1)} collective-permute-done((bf16[40,128]{1,0:T(8,128)(2,1)}, bf16[40,128]{1,0:T(8,128)(2,1)S(1)}, u32[]{:S(2)}, u32[]{:S(2)}) %collective-permute-start.2) | collective-permute-done | bytes 10272 | tf_op jit(solution)/shard_map/ppermute | solution.py:283
  12.8 6.7 %attend.1 = (bf16[8,32,128]{2,1,0:T(8,128)(2,1)}, bf16[32,128]{1,0:T(8,128)(2,1)S(1)}, bf16[32,128]{1,0:T(8,128)(2,1)S(1)}, bf16[32,128]{1,0:T(8,128)(2,1)S(1)}) custom-call(s32[4]{0:T(128)S(4)} %get-tuple-element.15.cache, s32[8,8]{1,0:T(8,128)} %page_hbm.1, s32[8]{0:T(128)} %length_hbm.1, bf16[8,32,128]{2,1,0:T(8,128)(2,1)} %bitcast.17, ...), custom_call_target="tpu_custom_call" | custom-call | tf_op jit(solution)/shard_map/attend/pallas_call | solution.py:284
  19.5 0.1 collective-permute-start.3
  19.6 0.7 %collective-permute-start.4 = (bf16[32,128]{1,0:T(8,128)(2,1)S(1)}, bf16[32,128]{1,0:T(8,128)(2,1)S(1)}, u32[]{:S(2)}, u32[]{:S(2)}) collective-permute-start(bf16[32,128]{1,0:T(8,128)(2,1)S(1)} %get-tuple-element.21), channel_id=1, source_target_pairs={{0,8},{4,12},{8,0},{12,4},{1,9},{5,13},{9,1},{13,5},{2,10},{6,14},... | collective-permute-start | bytes 24584 | tf_op jit(solution)/shard_map/ppermute | solution.py:314
  20.2 3.7 %collective-permute-start.5 = (bf16[32,128]{1,0:T(8,128)(2,1)S(1)}, bf16[32,128]{1,0:T(8,128)(2,1)S(1)}, u32[]{:S(2)}, u32[]{:S(2)}) collective-permute-start(bf16[32,128]{1,0:T(8,128)(2,1)S(1)} %get-tuple-element.22), channel_id=1, source_target_pairs={{0,12},{4,8},{8,4},{12,0},{1,13},{5,9},{9,5},{13,1},{2,14},{6,10},... | collective-permute-start | bytes 24584 | tf_op jit(solution)/shard_map/ppermute | solution.py:314
  24.0 0.0 collective-permute-done.3.refs_0_
  24.0 0.0 copy-start
  24.0 0.2 collective-permute-done.4.refs_1_
  24.2 0.0 copy-start.1
  24.2 1.5 %collective-permute-done.5.refs_2_ = bf16[32,128]{1,0:T(8,128)(2,1)S(1)} collective-permute-done((bf16[32,128]{1,0:T(8,128)(2,1)S(1)}, bf16[32,128]{1,0:T(8,128)(2,1)S(1)}, u32[]{:S(2)}, u32[]{:S(2)}) %collective-permute-start.5) | collective-permute-done | bytes 8224 | tf_op jit(solution)/shard_map/ppermute | solution.py:314
  25.7 0.0 copy-start.2
  25.7 0.0 copy-done
  25.7 0.0 copy-done.1
  25.7 0.6 %copy-done.2 = bf16[32,128]{1,0:T(8,128)(2,1)} copy-done((bf16[32,128]{1,0:T(8,128)(2,1)}, bf16[32,128]{1,0:T(8,128)(2,1)S(1)}, u32[]{:S(2)}) %copy-start.2) | copy-done | bytes 8216
  26.3 0.8 %place.1 = bf16[8,32,128]{2,1,0:T(8,128)(2,1)} custom-call(s32[4]{0:T(128)S(4)} %get-tuple-element.14.hidden, bf16[8,32,128]{2,1,0:T(8,128)(2,1)} %get-tuple-element.19.local, bf16[32,128]{1,0:T(8,128)(2,1)} %copy-done, bf16[32,128]{1,0:T(8,128)(2,1)} %copy-done.1, bf16[32,128]{1,0:T(8,128)(2,1)} %copy-done.2), custom_call_target="tpu_custom_call", output_to_operand_aliasing={{}: (1, {})} | custom-call | tf_op jit(solution)/shard_map/place/pallas_call | solution.py:315
Async XLA Ops:
  1.5 5.7 %collective-permute-start = (bf16[40,128]{1,0:T(8,128)(2,1)}, bf16[40,128]{1,0:T(8,128)(2,1)S(1)}, u32[]{:S(2)}, u32[]{:S(2)}) collective-permute-start(bf16[40,128]{1,0:T(8,128)(2,1)} %get-tuple-element.16), channel_id=1, source_target_pairs={{0,4},{4,0},{8,12},{12,8},{1,5},{5,1},{9,13},{13,9},{2,6},{6,2},{1... | collective-permute-start | bytes 30728 | tf_op jit(solution)/shard_map/ppermute | solution.py:283
  4.6 4.8 %collective-permute-start.1 = (bf16[40,128]{1,0:T(8,128)(2,1)}, bf16[40,128]{1,0:T(8,128)(2,1)S(1)}, u32[]{:S(2)}, u32[]{:S(2)}) collective-permute-start(bf16[40,128]{1,0:T(8,128)(2,1)} %get-tuple-element.17), channel_id=1, source_target_pairs={{0,8},{4,12},{8,0},{12,4},{1,9},{5,13},{9,1},{13,5},{2,10},{6,14},... | collective-permute-start | bytes 30728 | tf_op jit(solution)/shard_map/ppermute | solution.py:283
  7.2 5.7 %collective-permute-start.2 = (bf16[40,128]{1,0:T(8,128)(2,1)}, bf16[40,128]{1,0:T(8,128)(2,1)S(1)}, u32[]{:S(2)}, u32[]{:S(2)}) collective-permute-start(bf16[40,128]{1,0:T(8,128)(2,1)} %get-tuple-element.18), channel_id=1, source_target_pairs={{0,12},{4,8},{8,4},{12,0},{1,13},{5,9},{9,5},{13,1},{2,14},{6,10},... | collective-permute-start | bytes 30728 | tf_op jit(solution)/shard_map/ppermute | solution.py:283
  19.5 4.5 %collective-permute-start.3 = (bf16[32,128]{1,0:T(8,128)(2,1)S(1)}, bf16[32,128]{1,0:T(8,128)(2,1)S(1)}, u32[]{:S(2)}, u32[]{:S(2)}) collective-permute-start(bf16[32,128]{1,0:T(8,128)(2,1)S(1)} %get-tuple-element.20), channel_id=1, source_target_pairs={{0,4},{4,0},{8,12},{12,8},{1,5},{5,1},{9,13},{13,9},{2,6},{6,2},{1... | collective-permute-start | bytes 24584 | tf_op jit(solution)/shard_map/ppermute | solution.py:314
  19.6 4.6 %collective-permute-start.4 = (bf16[32,128]{1,0:T(8,128)(2,1)S(1)}, bf16[32,128]{1,0:T(8,128)(2,1)S(1)}, u32[]{:S(2)}, u32[]{:S(2)}) collective-permute-start(bf16[32,128]{1,0:T(8,128)(2,1)S(1)} %get-tuple-element.21), channel_id=1, source_target_pairs={{0,8},{4,12},{8,0},{12,4},{1,9},{5,13},{9,1},{13,5},{2,10},{6,14},... | collective-permute-start | bytes 24584 | tf_op jit(solution)/shard_map/ppermute | solution.py:314
  20.2 5.4 %collective-permute-start.5 = (bf16[32,128]{1,0:T(8,128)(2,1)S(1)}, bf16[32,128]{1,0:T(8,128)(2,1)S(1)}, u32[]{:S(2)}, u32[]{:S(2)}) collective-permute-start(bf16[32,128]{1,0:T(8,128)(2,1)S(1)} %get-tuple-element.22), channel_id=1, source_target_pairs={{0,12},{4,8},{8,4},{12,0},{1,13},{5,9},{9,5},{13,1},{2,14},{6,10},... | collective-permute-start | bytes 24584 | tf_op jit(solution)/shard_map/ppermute | solution.py:314
  24.0 1.7 %copy-start = (bf16[32,128]{1,0:T(8,128)(2,1)}, bf16[32,128]{1,0:T(8,128)(2,1)S(1)}, u32[]{:S(2)}) copy-start(bf16[32,128]{1,0:T(8,128)(2,1)S(1)} %collective-permute-done.3.refs_0_) | copy-start | bytes 24580
  24.2 1.5 %copy-start.1 = (bf16[32,128]{1,0:T(8,128)(2,1)}, bf16[32,128]{1,0:T(8,128)(2,1)S(1)}, u32[]{:S(2)}) copy-start(bf16[32,128]{1,0:T(8,128)(2,1)S(1)} %collective-permute-done.4.refs_1_) | copy-start | bytes 24580
  25.7 0.6 %copy-start.2 = (bf16[32,128]{1,0:T(8,128)(2,1)}, bf16[32,128]{1,0:T(8,128)(2,1)S(1)}, u32[]{:S(2)}) copy-start(bf16[32,128]{1,0:T(8,128)(2,1)S(1)} %collective-permute-done.5.refs_2_) | copy-start | bytes 24580
